TPU v7x, 256 devices: a whole 4x4x8 slice. The times are simulated.
256 devices in a mesh: mod: 8 (over y, x_hi), row: 32 (over z, x_lo, core).
Axes of the slice: x: 4 (x_hi: 2, x_lo: 2; x = x_hi * 2 + x_lo), y: 4, z: 8, core: 2. Of those that a mesh axis runs over, the one named last changes fastest.
Arguments:
- image: bfloat16 [6144, 1024], P('row', 'mod'), may hold values from -16 to 16
- modality: bfloat16 [8, 6144, 1024], P('mod', 'row'), may hold values from -16 to 16
- pair_index: int32 [8, 6144], P('mod'), may hold values from 0 to 6143, each once within a row
Outputs:
- image_grad: float32 [6144, 1024], P('row', 'mod')
- modality_grad: float32 [8, 6144, 1024], P('mod', 'row')
- row_loss: float32 [8, 6144], P('mod', 'row')
- col_loss: float32 [8, 6144], P('mod', 'row')
All inputs are finite; a program needn't handle non-finite values.
Results may differ from a plain program's by a relative error of at most 0.0015.
Values may be sent and summed in bfloat16 or wider, within the bound.
No kernel may reach another device: no remote copies, remote signals or barrier semaphores. Data moves between devices by JAX's collectives and lax.ppermute only.
A program may use at most 128 MiB of HBM per device.

v0:
```python
import jax
import jax.numpy as jnp
from jax import lax
from jax.sharding import PartitionSpec as P


def on_device(image, modality, pair_index):
    keys = modality[0]
    pairs = pair_index[0]
    rows = keys.shape[0]
    scale = keys.shape[1] ** (-0.5)
    start = lax.axis_index("row") * rows
    anchors = lax.all_gather(image, "mod", axis=1, tiled=True)
    all_keys = lax.all_gather(keys, "row", axis=0, tiled=True)
    batch = all_keys.shape[0]
    contract_last = (((1,), (1,)), ((), ()))
    contract_first = (((0,), (0,)), ((), ()))
    scores = (
        lax.dot_general(anchors, all_keys, contract_last, preferred_element_type=jnp.float32)
        * scale
    )
    columns = jnp.arange(batch, dtype=jnp.int32)
    my_pairs = lax.dynamic_slice_in_dim(pairs, start, rows)
    target = my_pairs[:, None] == columns[None, :]
    row_max = jnp.max(scores, axis=1)
    lse_row = row_max + jnp.log(jnp.sum(jnp.exp(scores - row_max[:, None]), axis=1))
    picked = jnp.where(target, scores, jnp.float32(0.0))
    row_loss = lse_row - jnp.sum(picked, axis=1)
    local_max = jnp.max(scores, axis=0)
    positive_part = jnp.sum(picked, axis=0)
    top = lax.pmax(local_max, "row")
    total, positive = lax.psum(
        (jnp.sum(jnp.exp(scores - top[None, :]), axis=0), positive_part), "row"
    )
    lse_col_all = top + jnp.log(total)
    col_loss = lax.dynamic_slice_in_dim(lse_col_all - positive, start, rows)
    weights = (
        jnp.exp(scores - lse_row[:, None])
        + jnp.exp(scores - lse_col_all[None, :])
        - jnp.where(target, jnp.float32(2.0), jnp.float32(0.0))
    ).astype(jnp.bfloat16)
    modality_grad = lax.psum_scatter(
        lax.dot_general(weights, anchors, contract_first, preferred_element_type=jnp.float32)
        * scale,
        "row",
        scatter_dimension=0,
        tiled=True,
    )
    image_term = jnp.dot(weights, all_keys, preferred_element_type=jnp.float32) * scale
    image_grad = lax.psum_scatter(image_term, "mod", scatter_dimension=1, tiled=True)
    return (image_grad, modality_grad[None], row_loss[None], col_loss[None])


def solution(mesh):
    in_specs = (P("row", "mod"), P("mod", "row", None), P("mod", None))
    out_specs = (P("row", "mod"), P("mod", "row", None), P("mod", "row"), P("mod", "row"))
    return jax.shard_map(
        on_device, mesh=mesh, in_specs=in_specs, out_specs=out_specs, check_vma=False
    )
```

profile of v0, /device:TPU:4, one launch (start us, length us, event | category | flops | bytes accessed | tf_op | source)
XLA Modules:
  0.0 688.1 jit_solution(6745541918703063121)
XLA Ops:
  7.2 0.0 copy-start
  7.2 0.0 all-gather.3.cloned.1.call-start
  7.2 0.7 all-gather.3.cloned.1.call-update
  7.9 0.0 reduce-scatter.3.cloned.1.call-start
  8.0 0.0 copy-done
  8.0 0.1 constant_dynamic-slice_fusion
  8.1 33.9 %all_gather.6 = bf16[192,1024]{1,0:T(8,128)(2,1)S(1)} all-gather(bf16[192,128]{1,0:T(8,128)(2,1)} %param.3), channel_id=1, replica_groups=mesh['mod'=8,'row'=32] {'mod'}, dimensions={1}, use_global_device_ids=true | all-gather | bytes 442368 | tf_op jit(solution)/shard_map/all_gather | solution.py:13
  41.9 52.8 %all-gather.3.cloned.1.call-done = bf16[1,6144,1024]{2,1,0:T(8,128)(2,1)} async-done(((bf16[1,192,1024]{2,1,0:T(8,128)(2,1)}), bf16[1,6144,1024]{2,1,0:T(8,128)(2,1)}) %all-gather.3.cloned.1.call-update) | async-done | bytes 12582928 | tf_op jit(solution)/shard_map/all_gather | solution.py:14
  94.7 11.0 %fusion.13 = (f32[192]{0:T(256)S(1)}, f32[6144]{0:T(1024)S(1)}, f32[192,6144]{1,0:T(8,128)}) fusion(bf16[192,1024]{1,0:T(8,128)(2,1)S(1)} %all_gather.6, bf16[1,6144,1024]{2,1,0:T(8,128)(2,1)} %all-gather.3.cloned.1.call-done), kind=kOutput, calls=%fused_computation.18 | convolution fusion | flops 2419451648 | bytes 17720064 | tf_op jit(solution)/shard_map/dot_general | solution.py:19
  105.7 108.3 %pmax.7 = f32[6144]{0:T(1024)S(1)} all-reduce(f32[6144]{0:T(1024)S(1)} %get-tuple-element.9), channel_id=1, replica_groups=mesh['mod'=8,'row'=32] {'row'}, use_global_device_ids=true, to_apply=%region_3.4 | all-reduce | flops 6144 | bytes 49152 | tf_op jit(solution)/shard_map/pmax | solution.py:31
  214.1 4.5 fusion.8
  218.5 104.4 %all-reduce = (f32[6144]{0:T(1024)S(1)}, f32[6144]{0:T(1024)S(1)}) all-reduce(f32[6144]{0:T(1024)S(1)} %get-tuple-element.6, f32[6144]{0:T(1024)S(1)} %get-tuple-element.4), channel_id=1, replica_groups=mesh['mod'=8,'row'=32] {'row'}, use_global_device_ids=true, to_apply=%region_5.6 | all-reduce | flops 12288 | bytes 98304 | tf_op jit(solution)/shard_map/psum | solution.py:32
  323.0 0.6 fusion.14
  323.6 10.3 %fusion.10 = f32[192,1024]{1,0:T(8,128)} fusion(bf16[1,6144,1024]{2,1,0:T(8,128)(2,1)} %all-gather.3.cloned.1.call-done, f32[192,6144]{1,0:T(8,128)} %get-tuple-element.14, s32[192]{0:T(256)S(1)} %bitcast.18, f32[6144]{0:T(1024)S(1)} %log_add_fusion, f32[192]{0:T(256)S(1)} %get-tuple-element.13), kind=kOutput, calls=%fused_computation.13 | convolution fusion | flops 2424373248 | bytes 18114048 | tf_op jit(solution)/shard_map/dot_general | solution.py:49
  333.9 0.0 reduce-scatter.3.cloned.1.call-update
  333.9 0.2 reduce-scatter.5.cloned.1.call-start
  334.1 15.4 %broadcast_multiply_fusion = f32[6144,1024]{1,0:T(8,128)} fusion(bf16[192,1024]{1,0:T(8,128)(2,1)S(1)} %all_gather.6, f32[192,6144]{1,0:T(8,128)} %get-tuple-element.14, s32[192]{0:T(256)S(1)} %bitcast.19, f32[6144]{0:T(1024)S(1)} %log_add_fusion, f32[192]{0:T(256)S(1)} %get-tuple-element.13), kind=kOutput, calls=%fused_computation.4 | convolution fusion | flops 2430468096 | bytes 30303744 | tf_op jit(solution)/shard_map/dot_general | solution.py:43
  349.5 0.0 reduce-scatter.5.cloned.1.call-update
  349.5 0.6 dynamic-slice_subtract_fusion
  350.2 56.4 %reduce-scatter.3.cloned.1.call-done = f32[192,128]{1,0:T(8,128)} async-done(((f32[192,1024]{1,0:T(8,128)}), f32[192,128]{1,0:T(8,128)}) %reduce-scatter.3.cloned.1.call-update) | async-done | bytes 98320 | tf_op jit(solution)/shard_map/reduce_scatter | solution.py:50
  406.6 275.0 %reduce-scatter.5.cloned.1.call-done = f32[192,1024]{1,0:T(8,128)} async-done(((f32[6144,1024]{1,0:T(8,128)}), f32[192,1024]{1,0:T(8,128)}) %reduce-scatter.5.cloned.1.call-update) | async-done | bytes 786448 | tf_op jit(solution)/shard_map/reduce_scatter | solution.py:42
  (1 shorter events, 0.0 us)
Async XLA Ops:
  7.2 0.8 copy-start
  7.2 87.5 %all-gather.3.cloned.1.call-start = ((), (), s32[]{:S(2)}) async-start(), calls=%async_computation.4 | async-start | bytes 12976128 | tf_op jit(solution)/shard_map/all_gather | solution.py:14
  7.9 398.7 %reduce-scatter.3.cloned.1.call-start = ((), (), s32[]{:S(2)}) async-start(), calls=%async_computation.2 | async-start | bytes 884736 | tf_op jit(solution)/shard_map/reduce_scatter | solution.py:50
  333.9 347.7 %reduce-scatter.5.cloned.1.call-start = ((), (), s32[]{:S(2)}) async-start(), calls=%async_computation.3 | async-start | bytes 25952256 | tf_op jit(solution)/shard_map/reduce_scatter | solution.py:42
Sparse Core Ops, SparseCore 0:
  9.9 84.8 all-gather.2
  334.0 72.5 reduce-scatter.2
  409.9 271.6 reduce-scatter.4
where the time goes:
time: 693 us; the launch traced here: 688 us
  waiting for transfers between devices  385 us (56%)
  blocking collectives  247 us (36%)
  matrix products  36.7 us (5%)
  between operations  13.8 us (2%)
    reduce_scatter x1, waiting for transfers between devices, on_device(): lax.psum_scatter(lax.dot_general(weights, anchors, contract_first, prefer...  275 us
    pmax x1, blocking collectives, on_device(): top = lax.pmax(local_max, 'row')  108 us
    psum x1, blocking collectives, on_device(): lax.psum((jnp.sum(jnp.exp(scores - top[None, :]), axis=0), positive_part)...  104 us
    reduce_scatter x1, waiting for transfers between devices, on_device(): lax.psum_scatter(image_term, 'mod', scatter_dimension=1, tiled=True)  56.4 us
    all_gather x1, waiting for transfers between devices, on_device(): all_keys = lax.all_gather(keys, 'row', axis=0, tiled=True)  52.8 us
    all_gather x1, blocking collectives, on_device(): anchors = lax.all_gather(image, 'mod', axis=1, tiled=True)  33.9 us
    dot_general x1, matrix products, on_device(): lax.dot_general(weights, anchors, contract_first, preferred_element_type=...  15.4 us
  transfers between devices with their start and end apart: 3, of which 3 were waited for; matrix products, arithmetic and copies ran while one was open for 2% of the time, Pallas kernels for 0%

commit v1 on v0

v1 whole, which is shorter than its diff:
```python
import functools
import jax
import jax.numpy as jnp
from jax import lax
from jax.experimental import pallas as pl
from jax.experimental.pallas import tpu as pltpu
from jax.sharding import Mesh, PartitionSpec as P

LAST = (((1,), (1,)), ((), ()))
FIRST = (((0,), (0,)), ((), ()))
F32, BF16, I16 = jnp.float32, jnp.bfloat16, jnp.int16
PAD = 16


def call(kernel, out, name, mib, **kw):
    return pl.pallas_call(
        kernel,
        out_shape=out,
        compiler_params=pltpu.CompilerParams(vmem_limit_bytes=mib * 2**20),
        cost_estimate=pl.CostEstimate(flops=1000, bytes_accessed=1000, transcendentals=0),
        name=name,
        **kw,
    )


def shape(s, t):
    return jax.ShapeDtypeStruct(s, t)


def eye(n):
    return lax.broadcasted_iota(jnp.int32, (n, n), 0) == lax.broadcasted_iota(jnp.int32, (n, n), 1)


def to_lanes(v):
    n = v.shape[0]
    parts = []
    for a in range(0, n, 128):
        w = min(128, n - a)
        parts.append(jnp.sum(jnp.where(eye(w), v[a : a + w], F32(0)), axis=0, keepdims=True))
    return jnp.concatenate(parts, axis=1)


def to_rows(v):
    n = v.shape[1]
    parts = []
    for a in range(0, n, 128):
        w = min(128, n - a)
        parts.append(jnp.sum(jnp.where(eye(w), v[:, a : a + w], F32(0)), axis=1, keepdims=True))
    return jnp.concatenate(parts, axis=0)


def power_of(x):
    top = jnp.max(jnp.abs(x), axis=0, keepdims=True)
    return jnp.ceil(jnp.log2(jnp.maximum(top, F32(1e-30)))) - 14.0


def fixed(x):
    return x.astype(jnp.int32).astype(I16)


def encode(x, ref):
    rows, cols = x.shape
    power = power_of(x)
    ref[:rows, :] = fixed(jnp.round(x * jnp.exp2(-power)))
    ref[rows:, :] = fixed(jnp.broadcast_to(power, (PAD, cols)))


def floats(c):
    return c.astype(jnp.int32).astype(F32)


def decode(c, tiles=1):
    f = floats(c)
    rows = c.shape[-2] - PAD
    n = rows // tiles
    parts = [f[..., i * n : (i + 1) * n, :] * jnp.exp2(f[..., rows + i : rows + i + 1, :]) for i in range(tiles)]
    return parts[0] if tiles == 1 else jnp.concatenate(parts, axis=-2)


def join_kernel(idx, after, *refs):
    del after
    keys, out = refs[:4], refs[4]
    rows = keys[0].shape[0]
    for d in range(4):
        out[pl.ds(pl.multiple_of((idx[0] ^ d) * rows, 16), rows), :] = keys[d][...]


def scores_kernel(scale, tile, idx, ks0, ks1, i0, i1, i3, ia, ib, pairs, cols, s_ref, im, rs, cs):
    y = idx[1]
    nzh, rows, width = ia.shape
    n_im = im.shape[0]
    half = ks0.shape[0]

    def place(k, xh, ref, first):
        at = pl.multiple_of((lax.rem(y + 4 - k, 4) * 2 + xh) * width, 128)
        for zh in range(nzh):
            im[zh * rows : (zh + 1) * rows, pl.ds(at, width)] = ref[first + zh]

    for k, ref in ((0, i0), (1, i1), (3, i3)):
        for xh in range(2):
            place(k, xh, ref, xh * nzh)
    place(2, 0, ia, 0)
    place(2, 1, ib, 0)

    rows_of = [slice(r, r + tile) for r in range(0, n_im, tile)]
    col_top, col_sum, col_pick = [None] * 2, [None] * 2, [None] * 2
    row_state = [None] * len(rows_of)

    def online(s, state, axis):
        top = jnp.max(s, axis=axis, keepdims=True)
        if state is None:
            return top, jnp.sum(jnp.exp(s - top), axis=axis, keepdims=True)
        new = jnp.maximum(state[0], top)
        return new, state[1] * jnp.exp(state[0] - new) + jnp.sum(jnp.exp(s - new), axis=axis, keepdims=True)

    def stats(h, r):
        lanes = slice(h * half, (h + 1) * half)
        s = s_ref[rows_of[r], lanes]
        picked = jnp.where(to_rows(pairs[:, rows_of[r]]) == cols[:, lanes], s, F32(0))
        old = row_state[r]
        top, total = online(s, old and old[:2], 1)
        pick = jnp.sum(picked, axis=1, keepdims=True)
        row_state[r] = (top, total, pick if old is None else old[2] + pick)
        state = None if col_top[h] is None else (col_top[h], col_sum[h])
        col_top[h], col_sum[h] = online(s, state, 0)
        pick = jnp.sum(picked, axis=0, keepdims=True)
        col_pick[h] = pick if col_pick[h] is None else col_pick[h] + pick

    before = None
    for h, ks in enumerate((ks0, ks1)):
        for r in range(len(rows_of)):
            s = lax.dot_general(im[rows_of[r], :], ks[...], LAST, preferred_element_type=F32)
            s_ref[rows_of[r], h * half : (h + 1) * half] = s * scale
            if before:
                stats(*before)
            before = (h, r)
    stats(*before)
    for r, (top, total, pick) in enumerate(row_state):
        rs[0:1, rows_of[r]] = to_lanes(top + jnp.log(total))
        rs[1:2, rows_of[r]] = to_lanes(pick)
    for h in range(2):
        cs[0:1, h * half : (h + 1) * half] = col_top[h] + jnp.log(col_sum[h])
        cs[1:2, h * half : (h + 1) * half] = col_pick[h]


def merge(parts):
    top = functools.reduce(jnp.maximum, parts)
    return top + jnp.log(sum(jnp.exp(p - top) for p in parts))


def meet(x, y):
    return jnp.concatenate([merge([x[0:1], y[0:1]]), x[1:2] + y[1:2]], axis=0)


def meet_first_kernel(c, c_other, r, r_other, c_out, r_out):
    half = c.shape[1] // 2
    other = c_other[...]
    c_out[...] = meet(c[...], jnp.concatenate([other[:, half:], other[:, :half]], axis=1))
    r_out[...] = meet(r[...], r_other[...])


def meet_kernel(a, b, out):
    out[...] = meet(a[...], b[...])


def weights_kernel(scale, tile, idx, r0, r1, c0, c1, pairs, cols, s_ref, ks0, ks1, w_ref, own, p1, p3, o2a, o2b, rl, cl, total):
    n_im, n_ks = s_ref.shape
    half = n_ks // 2
    width = own.shape[1]
    cstat = meet(c0[...], c1[...])
    lse_col = cstat[0:1]
    cl[...] = lse_col - cstat[1:2]
    rstat = meet(r0[...], r1[...])
    lse_row = rstat[0:1]
    rl[...] = lse_row - rstat[1:2]

    def weigh(a):
        rows = slice(a, a + tile)
        s = s_ref[rows, :]
        two = jnp.where(to_rows(pairs[:, rows]) == cols[...], F32(2), F32(0))
        w = jnp.exp(s - to_rows(lse_row[:, rows])) + jnp.exp(s - lse_col) - two
        w_ref[rows, :] = w.astype(BF16)

    def term(a):
        rows = slice(a, a + tile)
        x = jnp.dot(w_ref[rows, :half], ks0[...], preferred_element_type=F32)
        x += jnp.dot(w_ref[rows, half:], ks1[...], preferred_element_type=F32)
        total[rows, :] = x * scale

    tiles = range(0, n_im, tile)
    weigh(0)
    for a in tiles:
        if a + tile < n_im:
            weigh(a + tile)
        term(a)
    for k, out in ((2, None), (1, p1), (3, p3), (0, own)):
        lanes = pl.ds(pl.multiple_of(lax.rem(idx[1] + k, 4) * width, 128), width)
        if k == 2:
            encode(total[: n_im // 2, lanes], o2a)
            encode(total[n_im // 2 :, lanes], o2b)
        else:
            out[...] = total[:, lanes]


def relay_kernel(after, p1, p3, got_a, got_b, o1, o3):
    del after
    n = p1.shape[0] // 2
    encode(jnp.concatenate([p1[:n, :] + decode(got_a[...]), p1[n:, :]], axis=0), o1)
    encode(jnp.concatenate([p3[:n, :], p3[n:, :] + decode(got_b[...])], axis=0), o3)


def key_kernel(scale, w, im, own, out):
    half = w.shape[1] // 2
    rows = half // 4
    other = lax.dot_general(w[:, half:], im[...], FIRST, preferred_element_type=F32) * scale
    for p in range(4):
        encode(other[p * rows : (p + 1) * rows, :], out.at[p])
    own[...] = lax.dot_general(w[:, :half], im[...], FIRST, preferred_element_type=F32) * scale


def key_sum_kernel(idx, after, mine, got, own, *outs):
    del after
    rows = own.shape[0]
    for d in (3, 1, 2, 0):
        p = idx[0] ^ d
        x = mine[pl.ds(pl.multiple_of(p * rows, 16), rows), :] + decode(got[p])
        if d:
            encode(x, outs[d - 1])
        else:
            own[...] = x


def image_sum_kernel(after, own, *refs):
    del after
    got, out = refs[:-1], refs[-1]
    rows = out.shape[1] - PAD
    width = out.shape[2]
    n = out.shape[0] // 2
    total = own[...] + sum(decode(g[...]) for g in got)
    for xh in range(2):
        for zh in range(n):
            encode(total[zh * rows : (zh + 1) * rows, xh * width : (xh + 1) * width], out.at[xh * n + zh])


def shift(x, axis, n, k):
    return lax.ppermute(x, axis, [(i, (i + k) % n) for i in range(n)])


def flip(x, axis, n, d):
    return lax.ppermute(x, axis, [(i, i ^ d) for i in range(n)])


def on_device(image, modality, pair_index):
    keys = modality[0]
    rows, d = keys.shape
    width = image.shape[1]
    scale = d ** (-0.5)
    nzh = lax.axis_size("zh")
    zh, y, core = lax.axis_index("zh"), lax.axis_index("y"), lax.axis_index("core")
    zx = lax.axis_index(("zl", "xl"))
    t = lax.axis_index(("zl", "xl", "core"))
    n_im, n_ks = nzh * rows, 8 * rows
    half = n_ks // 2
    smem = pl.BlockSpec(memory_space=pltpu.SMEM)
    vmem = pl.BlockSpec(memory_space=pltpu.VMEM)
    late = pl.BlockSpec(memory_space=pl.ANY)
    idx = jnp.stack([zx, y]).astype(jnp.int32)

    def flip4(x, k):
        return flip(x, ("zl", "xl"), 4, k)

    same = [keys] + [flip4(keys, k) for k in (1, 2, 3)]
    i0 = lax.all_to_all(jnp.broadcast_to(image, (2 * nzh, rows, width)), ("xh", "zh"), 0, 0)
    i1, i3 = shift(i0, "y", 4, 1), shift(i0, "y", 4, 3)
    ia, ib = shift(i1[:nzh], "y", 4, 1), shift(i3[nzh:], "y", 4, 3)
    ks0 = call(join_kernel, shape((half, d), BF16), "join", 8, in_specs=[smem, late] + [vmem] * 4)(idx, i0, *same)
    ks1 = flip(ks0, "core", 2, 1)

    pairs = lax.dynamic_index_in_dim(pair_index.reshape(nzh, 8, rows), t, axis=1, keepdims=False)
    pairs = pairs.reshape(1, n_im).astype(F32)
    p = jnp.arange(n_ks, dtype=jnp.int32)
    cols = zh * n_ks + (p % half // rows * 2 + (core ^ (p // half))) * rows + p % rows
    cols = cols.reshape(1, n_ks).astype(F32)

    tile = min(256, n_im)
    scores, im, rs, cs = call(
        functools.partial(scores_kernel, scale, tile),
        [shape((n_im, n_ks), F32), shape((n_im, d), BF16), shape((2, n_im), F32), shape((2, n_ks), F32)],
        "scores",
        28,
        in_specs=[smem] + [vmem] * 9,
    )(idx, ks0, ks1, i0, i1, i3, ia, ib, pairs, cols)
    cs, rs = call(meet_first_kernel, [shape((2, n_ks), F32), shape((2, n_im), F32)], "meet", 4, in_specs=[vmem] * 4)(
        cs, flip(cs, "core", 2, 1), rs, flip(rs, "zh", 4, 1)
    )
    rs_other = flip(rs, "zh", 4, 3)
    cs = call(meet_kernel, shape((2, n_ks), F32), "meet_x", 4, in_specs=[vmem] * 2)(cs, flip(cs, "xl", 2, 1))
    cs_other = flip(cs, "zl", 2, 1)
    outs = [shape((n_im, n_ks), BF16)] + [shape((n_im, 2 * width), F32)] * 3
    outs += [shape((n_im // 2 + PAD, 2 * width), I16)] * 2 + [shape((1, n_im), F32), shape((1, n_ks), F32)]
    weights, own, p1, p3, q2a, q2b, row_loss, col_loss = call(
        functools.partial(weights_kernel, scale, tile),
        outs,
        "weights",
        28,
        in_specs=[smem] + [vmem] * 9,
        scratch_shapes=[pltpu.VMEM((n_im, d), F32)],
    )(idx, rs, rs_other, cs, cs_other, pairs, cols, scores, ks0, ks1)
    q2a, q2b = shift(q2a, "y", 4, 1), shift(q2b, "y", 4, 3)
    mine, sent = call(
        functools.partial(key_kernel, scale),
        [shape((half, d), F32), shape((4, rows + PAD, d), I16)],
        "key_term",
        24,
        in_specs=[vmem] * 2,
    )(weights, im)
    got = flip(sent, "core", 2, 1)
    q1, q3 = call(
        relay_kernel,
        [shape((n_im + PAD, 2 * width), I16)] * 2,
        "relay",
        12,
        in_specs=[late] + [vmem] * 4,
    )(mine, p1, p3, q2a, q2b)
    own_key, *pieces = call(
        key_sum_kernel,
        [shape((rows, d), F32)] + [shape((rows + PAD, d), I16)] * 3,
        "key_sum",
        16,
        in_specs=[smem, late] + [vmem] * 2,
    )(idx, q1, mine, got)
    q1, q3 = shift(q1, "y", 4, 1), shift(q3, "y", 4, 3)
    pieces = [flip4(x, k + 1) for k, x in enumerate(pieces)]
    eighths = call(
        image_sum_kernel,
        shape((2 * nzh, rows + PAD, width), I16),
        "image_sum",
        12,
        in_specs=[late] + [vmem] * 3,
    )(own_key, own, q1, q3)
    eighths = lax.all_to_all(eighths, ("xh", "zh"), 0, 0)
    modality_grad = own_key + sum(decode(x) for x in pieces)
    image_grad = jnp.sum(decode(eighths), axis=0)
    row_loss = lax.dynamic_slice_in_dim(row_loss, zh * rows, rows, axis=1)
    col_loss = lax.dynamic_slice_in_dim(col_loss, zx * rows, rows, axis=1)
    return (image_grad, modality_grad[None], row_loss, col_loss)


def solution(mesh):
    ny = mesh.devices.shape[0] // 2
    nzh = mesh.devices.shape[1] // 8
    names = ("y", "xh", "zh", "zl", "xl", "core")
    fine = Mesh(mesh.devices.reshape(ny, 2, nzh, 2, 2, 2), names)
    mod, rows = names[:2], names[2:]
    in_specs = (P(rows, mod), P(mod, rows, None), P(mod, None))
    out_specs = (P(rows, mod), P(mod, rows, None), P(mod, rows), P(mod, rows))
    return jax.shard_map(
        on_device, mesh=fine, in_specs=in_specs, out_specs=out_specs, check_vma=False
    )
```

time: 693 us -> 166 us (0.24)
  waiting for transfers between devices: 385 us -> 83 us
  blocking collectives: 247 us -> 0 us
  starting transfers between devices: 0.3 us -> 47.5 us
  matrix products: 36.7 us -> 0 us
  Pallas kernels: 0 us -> 19.1 us
  between operations: 13.8 us -> 0.83 us
  local copies, waits for them, and re-layouts: 0.09 us -> 9.43 us
    reduce_scatter x2 -> x0, waiting for transfers between devices: 331 us -> none  [the longest x1 275 us: on_device(): lax.psum_scatter(lax.dot_general(weights, anchors, contract_first, prefer...]
    pmax x1 -> x0, blocking collectives: 108 us -> none  [on_device(): top = lax.pmax(local_max, 'row')]
    psum x1 -> x0, blocking collectives: 104 us -> none  [on_device(): lax.psum((jnp.sum(jnp.exp(scores - top[None, :]), axis=0), positive_part)...]
    ppermute x0 -> x21, waiting for transfers between devices: none -> 82.9 us  [the longest x13 55.6 us: flip(): return lax.ppermute(x, axis, [(i, i ^ d) for i in range(n)])]
    all_gather x1 -> x0, waiting for transfers between devices: 52.8 us -> none  [on_device(): all_keys = lax.all_gather(keys, 'row', axis=0, tiled=True)]
    dot_general x3 -> x0, matrix products: 36.7 us -> none  [the longest x1 15.4 us: on_device(): lax.dot_general(weights, anchors, contract_first, preferred_element_type=...]
    all_gather x1 -> x0, blocking collectives: 33.9 us -> none  [on_device(): anchors = lax.all_gather(image, 'mod', axis=1, tiled=True)]
    ppermute x0 -> x21, starting transfers between devices: none -> 27.5 us  [the longest x13 14.1 us: flip(): return lax.ppermute(x, axis, [(i, i ^ d) for i in range(n)])]
  transfers between devices with their start and end apart: 3 -> 23, of which waited for: 3 -> 13; matrix products, arithmetic and copies ran while one was open for 2% -> 6% of each run, Pallas kernels for 0% -> 1%
where the time goes in v1:
time: 166 us; the launch traced here: 165 us
  waiting for transfers between devices  83 us (50%)
  starting transfers between devices  47.5 us (29%)
  Pallas kernels  19.1 us (12%)
  local copies, waits for them, and re-layouts  9.43 us (6%)
  other arithmetic  5.67 us (3%)
    ppermute x13, waiting for transfers between devices, flip(): return lax.ppermute(x, axis, [(i, i ^ d) for i in range(n)])  55.6 us
    ppermute x8, waiting for transfers between devices, shift(): return lax.ppermute(x, axis, [(i, (i + k) % n) for i in range(n)])  27.3 us
    ppermute x13, starting transfers between devices, flip(): return lax.ppermute(x, axis, [(i, i ^ d) for i in range(n)])  14.1 us
    ppermute x8, starting transfers between devices, shift(): return lax.ppermute(x, axis, [(i, (i + k) % n) for i in range(n)])  13.3 us
    all_to_all x1, starting transfers between devices, on_device(): lax.all_to_all(jnp.broadcast_to(image, (2 * nzh, rows, width)), ('xh', 'z...  11.4 us
    all_to_all x1, starting transfers between devices, on_device(): eighths = lax.all_to_all(eighths, ('xh', 'zh'), 0, 0)  8.6 us
    pallas_call x1, Pallas kernels, on_device(): call(functools.partial(scores_kernel, scale, tile), [shape((n_im, n_ks),...  6.07 us
    pallas_call x1, Pallas kernels, on_device(): call(functools.partial(weights_kernel, scale, tile), outs, 'weights', 28,...  4.96 us
  transfers between devices with their start and end apart: 23, of which 13 were waited for; matrix products, arithmetic and copies ran while one was open for 6% of the time, Pallas kernels for 1%

profile of v1, /device:TPU:4, one launch (start us, length us, event | category | flops | bytes accessed | tf_op | source)
XLA Modules:
  0.0 165.5 jit_solution(7418437590362469081)
XLA Ops:
  0.6 1.6 broadcast_in_dim.6
  2.2 11.4 %all-to-all-start = ((bf16[8,192,128]{2,1,0:T(8,128)(2,1)}), bf16[8,192,128]{2,1,0:T(8,128)(2,1)S(1)}, u32[]{:S(2)}, u32[]{:S(2)}) async-start(bf16[8,192,128]{2,1,0:T(8,128)(2,1)} %broadcast_in_dim.6), calls=%async_computation | async-start | bytes 786432 | tf_op jit(solution)/shard_map/all_to_all | solution.py:273
  13.7 1.7 collective-permute-start.2
  17.2 17.6 %collective-permute-done.2.refs_3_ = bf16[192,1024]{1,0:T(8,128)(2,1)S(1)} collective-permute-done((bf16[192,1024]{1,0:T(8,128)(2,1)}, bf16[192,1024]{1,0:T(8,128)(2,1)S(1)}, u32[]{:S(2)}, u32[]{:S(2)}) %collective-permute-start.2) | collective-permute-done | bytes 393248 | tf_op jit(solution)/shard_map/ppermute | solution.py:250
  34.8 6.4 %collective-permute-done.1.refs_2_ = bf16[192,1024]{1,0:T(8,128)(2,1)S(1)} collective-permute-done((bf16[192,1024]{1,0:T(8,128)(2,1)}, bf16[192,1024]{1,0:T(8,128)(2,1)S(1)}, u32[]{:S(2)}, u32[]{:S(2)}) %collective-permute-start.1) | collective-permute-done | bytes 393248 | tf_op jit(solution)/shard_map/ppermute | solution.py:250
  43.0 3.1 %collective-permute-start.5 = (bf16[8,192,128]{2,1,0:T(8,128)(2,1)S(1)}, bf16[8,192,128]{2,1,0:T(8,128)(2,1)}, u32[]{:S(2)}, u32[]{:S(2)}) collective-permute-start(bf16[8,192,128]{2,1,0:T(8,128)(2,1)S(1)} %all-to-all-done.after.i0), channel_id=1, source_target_pairs={{0,192},{64,0},{128,64},{192,128},{1,193},{65,1},{129,65},{193,129... | collective-permute-start | bytes 1179656 | tf_op jit(solution)/shard_map/ppermute | solution.py:246
  46.6 2.0 %reduce.3 = s32[6144]{0:T(1024)} reduce(s32[1,6144]{1,0:T(1,128)} %param.5, s32[]{:T(128)} %broadcast.157), dimensions={0}, to_apply=%param.5.reduce_sub_computation.3 | reduce | bytes 49156 | tf_op args[2]
  48.6 1.4 reshape.140
  50.9 4.1 %collective-permute-done.5.i3 = bf16[8,192,128]{2,1,0:T(8,128)(2,1)} collective-permute-done((bf16[8,192,128]{2,1,0:T(8,128)(2,1)S(1)}, bf16[8,192,128]{2,1,0:T(8,128)(2,1)}, u32[]{:S(2)}, u32[]{:S(2)}) %collective-permute-start.5) | collective-permute-done | bytes 393248 | tf_op jit(solution)/shard_map/ppermute | solution.py:246
  56.0 3.9 %collective-permute-start.7 = (bf16[4,192,128]{2,1,0:T(8,128)(2,1)S(1)}, bf16[4,192,128]{2,1,0:T(8,128)(2,1)S(1)}, u32[]{:S(2)}, u32[]{:S(2)}) collective-permute-start(bf16[4,192,128]{2,1,0:T(8,128)(2,1)S(1)} %slice.41), channel_id=1, source_target_pairs={{0,192},{64,0},{128,64},{192,128},{1,193},{65,1},{129,65},{193,129... | collective-permute-start | bytes 589832 | tf_op jit(solution)/shard_map/ppermute | solution.py:246
  61.0 2.8 %collective-permute-done.7.ib = bf16[4,192,128]{2,1,0:T(8,128)(2,1)S(1)} collective-permute-done((bf16[4,192,128]{2,1,0:T(8,128)(2,1)S(1)}, bf16[4,192,128]{2,1,0:T(8,128)(2,1)S(1)}, u32[]{:S(2)}, u32[]{:S(2)}) %collective-permute-start.7) | collective-permute-done | bytes 196640 | tf_op jit(solution)/shard_map/ppermute | solution.py:246
  63.8 4.4 %collective-permute-done.6.ia = bf16[4,192,128]{2,1,0:T(8,128)(2,1)S(1)} collective-permute-done((bf16[4,192,128]{2,1,0:T(8,128)(2,1)S(1)}, bf16[4,192,128]{2,1,0:T(8,128)(2,1)S(1)}, u32[]{:S(2)}, u32[]{:S(2)}) %collective-permute-start.6) | collective-permute-done | bytes 196640 | tf_op jit(solution)/shard_map/ppermute | solution.py:246
  68.3 6.1 %scores.1 = (f32[768,1536]{1,0:T(8,128)S(1)}, bf16[768,1024]{1,0:T(8,128)(2,1)S(1)}, f32[2,768]{1,0:T(2,128)S(1)}, f32[2,1536]{1,0:T(2,128)S(1)}) custom-call(s32[2]{0:T(128)S(1)} %pad_add_fusion.idx, bf16[768,1024]{1,0:T(8,128)(2,1)S(1)} %join.1.ks0, bf16[768,1024]{1,0:T(8,128)(2,1)S(1)} %collective-permute-done.3.ks1, ...), custom_call_target="tpu_custom_call" | custom-call | flops 1000 | bytes 1000 | tf_op jit(solution)/shard_map/scores/pallas_call | solution.py:286
  74.4 1.6 collective-permute-start.9
  76.0 3.0 %collective-permute-done.9.r_other = f32[2,768]{1,0:T(2,128)S(1)} collective-permute-done((f32[2,768]{1,0:T(2,128)S(1)}, f32[2,768]{1,0:T(2,128)S(1)}, u32[]{:S(2)}, u32[]{:S(2)}) %collective-permute-start.9) | collective-permute-done | bytes 6176 | tf_op jit(solution)/shard_map/ppermute | solution.py:250
  79.1 1.5 collective-permute-start.11
  80.6 2.5 %collective-permute-done.11.b = f32[2,1536]{1,0:T(2,128)S(1)} collective-permute-done((f32[2,1536]{1,0:T(2,128)S(1)}, f32[2,1536]{1,0:T(2,128)S(1)}, u32[]{:S(2)}, u32[]{:S(2)}) %collective-permute-start.11) | collective-permute-done | bytes 12320 | tf_op jit(solution)/shard_map/ppermute | solution.py:250
  83.8 3.1 %collective-permute-start.10 = (f32[2,768]{1,0:T(2,128)S(1)}, f32[2,768]{1,0:T(2,128)S(1)}, u32[]{:S(2)}, u32[]{:S(2)}) collective-permute-start(f32[2,768]{1,0:T(2,128)S(1)} %get-tuple-element.28.r0), channel_id=1, source_target_pairs={{0,24},{8,16},{16,8},{24,0},{1,25},{9,17},{17,9},{25,1},{2,26},{10... | collective-permute-start | bytes 18440 | tf_op jit(solution)/shard_map/ppermute | solution.py:250
  86.9 2.6 %collective-permute-done.10.r1 = f32[2,768]{1,0:T(2,128)S(1)} collective-permute-done((f32[2,768]{1,0:T(2,128)S(1)}, f32[2,768]{1,0:T(2,128)S(1)}, u32[]{:S(2)}, u32[]{:S(2)}) %collective-permute-start.10) | collective-permute-done | bytes 6176 | tf_op jit(solution)/shard_map/ppermute | solution.py:250
  89.6 5.0 %weights.1 = (bf16[768,1536]{1,0:T(8,128)(2,1)S(1)}, f32[768,256]{1,0:T(8,128)S(1)}, f32[768,256]{1,0:T(8,128)S(1)}, f32[768,256]{1,0:T(8,128)S(1)}, s16[400,256...) custom-call(s32[2]{0:T(128)S(1)} %pad_add_fusion.idx, ...), custom_call_target="tpu_custom_call" | custom-call | flops 1000 | bytes 1000 | tf_op jit(solution)/shard_map/weights/pallas_call | solution.py:301
  94.5 3.1 %key_term.1 = (f32[768,1024]{1,0:T(8,128)S(1)}, s16[4,208,1024]{2,1,0:T(8,128)(2,1)S(1)}) custom-call(bf16[768,1536]{1,0:T(8,128)(2,1)S(1)} %get-tuple-element.31.w, bf16[768,1024]{1,0:T(8,128)(2,1)S(1)} %get-tuple-element.32.im), custom_call_target="tpu_custom_call" | custom-call | flops 1000 | bytes 1000 | tf_op jit(solution)/shard_map/key_term/pallas_call | solution.py:310
  97.9 3.2 %collective-permute-start.14 = (s16[400,256]{1,0:T(8,128)(2,1)S(1)}, s16[400,256]{1,0:T(8,128)(2,1)S(1)}, u32[]{:S(2)}, u32[]{:S(2)}) collective-permute-start(s16[400,256]{1,0:T(8,128)(2,1)S(1)} %get-tuple-element.37), channel_id=1, source_target_pairs={{0,192},{64,0},{128,64},{192,128},{1,193},{65,1},{129,65},{193,129... | collective-permute-start | bytes 614408 | tf_op jit(solution)/shard_map/ppermute | solution.py:246
  101.1 5.4 %collective-permute-done.13.got_a = s16[400,256]{1,0:T(8,128)(2,1)S(1)} collective-permute-done((s16[400,256]{1,0:T(8,128)(2,1)S(1)}, s16[400,256]{1,0:T(8,128)(2,1)S(1)}, u32[]{:S(2)}, u32[]{:S(2)}) %collective-permute-start.13) | collective-permute-done | bytes 204832 | tf_op jit(solution)/shard_map/ppermute | solution.py:246
  107.6 2.0 %key_sum.1 = (f32[192,1024]{1,0:T(8,128)S(1)}, s16[208,1024]{1,0:T(8,128)(2,1)}, s16[208,1024]{1,0:T(8,128)(2,1)S(1)}, s16[208,1024]{1,0:T(8,128)(2,1)S(1)}) custom-call(s32[2]{0:T(128)S(1)} %pad_add_fusion.idx, s16[784,256]{1,0:T(8,128)(2,1)S(1)} %get-tuple-element.38.after, f32[768,1024]{1,0:T(8,128)S(1)} %get-tuple-element.33.after.mine, ...), custom_call_target="tpu_custom_call" | custom-call | flops 1000 | bytes 1000 | tf_op jit(solution)/shard_map/key_sum/pallas_call | solution.py:325
  112.4 3.0 %collective-permute-start.17 = (s16[784,256]{1,0:T(8,128)(2,1)}, s16[784,256]{1,0:T(8,128)(2,1)S(1)}, u32[]{:S(2)}, u32[]{:S(2)}) collective-permute-start(s16[784,256]{1,0:T(8,128)(2,1)} %get-tuple-element.42), channel_id=1, source_target_pairs={{0,192},{64,0},{128,64},{192,128},{1,193},{65,1},{129,65},{193,129... | collective-permute-start | bytes 1204232 | tf_op jit(solution)/shard_map/ppermute | solution.py:246
  116.0 7.4 %collective-permute-done.17.refs_1_ = s16[784,256]{1,0:T(8,128)(2,1)S(1)} collective-permute-done((s16[784,256]{1,0:T(8,128)(2,1)}, s16[784,256]{1,0:T(8,128)(2,1)S(1)}, u32[]{:S(2)}, u32[]{:S(2)}) %collective-permute-start.17) | collective-permute-done | bytes 401440 | tf_op jit(solution)/shard_map/ppermute | solution.py:246
  123.4 3.1 %collective-permute-done.16.refs_0_ = s16[784,256]{1,0:T(8,128)(2,1)S(1)} collective-permute-done((s16[784,256]{1,0:T(8,128)(2,1)S(1)}, s16[784,256]{1,0:T(8,128)(2,1)S(1)}, u32[]{:S(2)}, u32[]{:S(2)}) %collective-permute-start.16) | collective-permute-done | bytes 401440 | tf_op jit(solution)/shard_map/ppermute | solution.py:246
  127.6 8.6 %all-to-all-start.1 = ((s16[8,208,128]{2,1,0:T(8,128)(2,1)}), s16[8,208,128]{2,1,0:T(8,128)(2,1)S(1)}, u32[]{:S(2)}, u32[]{:S(2)}) async-start(s16[8,208,128]{2,1,0:T(8,128)(2,1)} %image_sum.1), calls=%async_computation.1 | async-start | bytes 851968 | tf_op jit(solution)/shard_map/all_to_all | solution.py:341
  137.2 1.3 collective-permute-start.20
  139.7 16.8 %collective-permute-done.19 = s16[208,1024]{1,0:T(8,128)(2,1)S(1)} collective-permute-done((s16[208,1024]{1,0:T(8,128)(2,1)S(1)}, s16[208,1024]{1,0:T(8,128)(2,1)S(1)}, u32[]{:S(2)}, u32[]{:S(2)}) %collective-permute-start.19) | collective-permute-done | bytes 426016 | tf_op jit(solution)/shard_map/ppermute | solution.py:250
  156.6 6.7 %collective-permute-done.20 = s16[208,1024]{1,0:T(8,128)(2,1)S(1)} collective-permute-done((s16[208,1024]{1,0:T(8,128)(2,1)S(1)}, s16[208,1024]{1,0:T(8,128)(2,1)S(1)}, u32[]{:S(2)}, u32[]{:S(2)}) %collective-permute-start.20) | collective-permute-done | bytes 426016 | tf_op jit(solution)/shard_map/ppermute | solution.py:250
  163.4 1.2 fusion.2
  (59 shorter events, 17.0 us)
Async XLA Ops:
  2.2 39.0 %all-to-all-start = ((bf16[8,192,128]{2,1,0:T(8,128)(2,1)}), bf16[8,192,128]{2,1,0:T(8,128)(2,1)S(1)}, u32[]{:S(2)}, u32[]{:S(2)}) async-start(bf16[8,192,128]{2,1,0:T(8,128)(2,1)} %broadcast_in_dim.6), calls=%async_computation | async-start | bytes 786432 | tf_op jit(solution)/shard_map/all_to_all | solution.py:273
  13.7 21.2 %collective-permute-start.2 = (bf16[192,1024]{1,0:T(8,128)(2,1)}, bf16[192,1024]{1,0:T(8,128)(2,1)S(1)}, u32[]{:S(2)}, u32[]{:S(2)}) collective-permute-start(bf16[192,1024]{1,0:T(8,128)(2,1)} %bitcast.11), channel_id=1, source_target_pairs={{0,6},{2,4},{4,2},{6,0},{1,7},{3,5},{5,3},{7,1},{8,14},{10,12},{12... | collective-permute-start | bytes 1179656 | tf_op jit(solution)/shard_map/ppermute | solution.py:250
  15.3 25.9 %collective-permute-start.1 = (bf16[192,1024]{1,0:T(8,128)(2,1)}, bf16[192,1024]{1,0:T(8,128)(2,1)S(1)}, u32[]{:S(2)}, u32[]{:S(2)}) collective-permute-start(bf16[192,1024]{1,0:T(8,128)(2,1)} %bitcast.12), channel_id=1, source_target_pairs={{0,4},{2,6},{4,0},{6,2},{1,5},{3,7},{5,1},{7,3},{8,12},{10,14},{12... | collective-permute-start | bytes 1179656 | tf_op jit(solution)/shard_map/ppermute | solution.py:250
  16.3 24.9 %collective-permute-start = (bf16[192,1024]{1,0:T(8,128)(2,1)}, bf16[192,1024]{1,0:T(8,128)(2,1)S(1)}, u32[]{:S(2)}, u32[]{:S(2)}) collective-permute-start(bf16[192,1024]{1,0:T(8,128)(2,1)} %bitcast.13), channel_id=1, source_target_pairs={{0,2},{2,0},{4,6},{6,4},{1,3},{3,1},{5,7},{7,5},{8,10},{10,8},{12,... | collective-permute-start | bytes 1179656 | tf_op jit(solution)/shard_map/ppermute | solution.py:250
  41.2 1.0 copy-start.2
  42.9 25.4 %collective-permute-start.3 = (bf16[768,1024]{1,0:T(8,128)(2,1)S(1)}, bf16[768,1024]{1,0:T(8,128)(2,1)S(1)}, u32[]{:S(2)}, u32[]{:S(2)}) collective-permute-start(bf16[768,1024]{1,0:T(8,128)(2,1)S(1)} %join.1.ks0), channel_id=1, source_target_pairs={{0,1},{1,0},{2,3},{3,2},{4,5},{5,4},{6,7},{7,6},{8,9},{9,8},{10,11... | collective-permute-start | bytes 4718600 | tf_op jit(solution)/shard_map/ppermute | solution.py:250
  43.0 12.1 %collective-permute-start.5 = (bf16[8,192,128]{2,1,0:T(8,128)(2,1)S(1)}, bf16[8,192,128]{2,1,0:T(8,128)(2,1)}, u32[]{:S(2)}, u32[]{:S(2)}) collective-permute-start(bf16[8,192,128]{2,1,0:T(8,128)(2,1)S(1)} %all-to-all-done.after.i0), channel_id=1, source_target_pairs={{0,192},{64,0},{128,64},{192,128},{1,193},{65,1},{129,65},{193,129... | collective-permute-start | bytes 1179656 | tf_op jit(solution)/shard_map/ppermute | solution.py:246
  46.1 13.8 %collective-permute-start.4 = (bf16[8,192,128]{2,1,0:T(8,128)(2,1)S(1)}, bf16[8,192,128]{2,1,0:T(8,128)(2,1)}, u32[]{:S(2)}, u32[]{:S(2)}) collective-permute-start(bf16[8,192,128]{2,1,0:T(8,128)(2,1)S(1)} %all-to-all-done.after.i0), channel_id=1, source_target_pairs={{0,64},{64,128},{128,192},{192,0},{1,65},{65,129},{129,193},{193,1... | collective-permute-start | bytes 1179656 | tf_op jit(solution)/shard_map/ppermute | solution.py:246
  56.0 7.8 %collective-permute-start.7 = (bf16[4,192,128]{2,1,0:T(8,128)(2,1)S(1)}, bf16[4,192,128]{2,1,0:T(8,128)(2,1)S(1)}, u32[]{:S(2)}, u32[]{:S(2)}) collective-permute-start(bf16[4,192,128]{2,1,0:T(8,128)(2,1)S(1)} %slice.41), channel_id=1, source_target_pairs={{0,192},{64,0},{128,64},{192,128},{1,193},{65,1},{129,65},{193,129... | collective-permute-start | bytes 589832 | tf_op jit(solution)/shard_map/ppermute | solution.py:246
  60.8 7.5 %collective-permute-start.6 = (bf16[4,192,128]{2,1,0:T(8,128)(2,1)S(1)}, bf16[4,192,128]{2,1,0:T(8,128)(2,1)S(1)}, u32[]{:S(2)}, u32[]{:S(2)}) collective-permute-start(bf16[4,192,128]{2,1,0:T(8,128)(2,1)S(1)} %slice.40), channel_id=1, source_target_pairs={{0,64},{64,128},{128,192},{192,0},{1,65},{65,129},{129,193},{193,1... | collective-permute-start | bytes 589832 | tf_op jit(solution)/shard_map/ppermute | solution.py:246
  74.3 4.7 %collective-permute-start.8 = (f32[2,1536]{1,0:T(2,128)S(1)}, f32[2,1536]{1,0:T(2,128)S(1)}, u32[]{:S(2)}, u32[]{:S(2)}) collective-permute-start(f32[2,1536]{1,0:T(2,128)S(1)} %get-tuple-element.26.c), channel_id=1, source_target_pairs={{0,1},{1,0},{2,3},{3,2},{4,5},{5,4},{6,7},{7,6},{8,9},{9,8},{10,11... | collective-permute-start | bytes 36872 | tf_op jit(solution)/shard_map/ppermute | solution.py:250
  74.4 4.6 %collective-permute-start.9 = (f32[2,768]{1,0:T(2,128)S(1)}, f32[2,768]{1,0:T(2,128)S(1)}, u32[]{:S(2)}, u32[]{:S(2)}) collective-permute-start(f32[2,768]{1,0:T(2,128)S(1)} %get-tuple-element.27.r), channel_id=1, source_target_pairs={{0,8},{8,0},{16,24},{24,16},{1,9},{9,1},{17,25},{25,17},{2,10},{10... | collective-permute-start | bytes 18440 | tf_op jit(solution)/shard_map/ppermute | solution.py:250
  79.1 4.0 %collective-permute-start.11 = (f32[2,1536]{1,0:T(2,128)S(1)}, f32[2,1536]{1,0:T(2,128)S(1)}, u32[]{:S(2)}, u32[]{:S(2)}) collective-permute-start(f32[2,1536]{1,0:T(2,128)S(1)} %get-tuple-element.29.a), channel_id=1, source_target_pairs={{0,2},{2,0},{1,3},{3,1},{4,6},{6,4},{5,7},{7,5},{8,10},{10,8},{9,1... | collective-permute-start | bytes 36872 | tf_op jit(solution)/shard_map/ppermute | solution.py:250
  83.1 6.5 %collective-permute-start.12 = (f32[2,1536]{1,0:T(2,128)S(1)}, f32[2,1536]{1,0:T(2,128)S(1)}, u32[]{:S(2)}, u32[]{:S(2)}) collective-permute-start(f32[2,1536]{1,0:T(2,128)S(1)} %meet_x.1.c0), channel_id=1, source_target_pairs={{0,4},{4,0},{1,5},{5,1},{2,6},{6,2},{3,7},{7,3},{8,12},{12,8},{9,1... | collective-permute-start | bytes 36872 | tf_op jit(solution)/shard_map/ppermute | solution.py:250
  83.8 5.7 %collective-permute-start.10 = (f32[2,768]{1,0:T(2,128)S(1)}, f32[2,768]{1,0:T(2,128)S(1)}, u32[]{:S(2)}, u32[]{:S(2)}) collective-permute-start(f32[2,768]{1,0:T(2,128)S(1)} %get-tuple-element.28.r0), channel_id=1, source_target_pairs={{0,24},{8,16},{16,8},{24,0},{1,25},{9,17},{17,9},{25,1},{2,26},{10... | collective-permute-start | bytes 18440 | tf_op jit(solution)/shard_map/ppermute | solution.py:250
  94.5 3.1 %copy-start = (f32[768,256]{1,0:T(8,128)}, f32[768,256]{1,0:T(8,128)S(1)}, u32[]{:S(2)}) copy-start(f32[768,256]{1,0:T(8,128)S(1)} %get-tuple-element.41.own) | copy-start | bytes 2359300
  97.7 9.9 %collective-permute-start.15 = (s16[4,208,1024]{2,1,0:T(8,128)(2,1)S(1)}, s16[4,208,1024]{2,1,0:T(8,128)(2,1)S(1)}, u32[]{:S(2)}, u32[]{:S(2)}) collective-permute-start(s16[4,208,1024]{2,1,0:T(8,128)(2,1)S(1)} %get-tuple-element.39), channel_id=1, source_target_pairs={{0,1},{1,0},{2,3},{3,2},{4,5},{5,4},{6,7},{7,6},{8,9},{9,8},{10,11... | collective-permute-start | bytes 5111816 | tf_op jit(solution)/shard_map/ppermute | solution.py:250
  97.8 8.7 %collective-permute-start.13 = (s16[400,256]{1,0:T(8,128)(2,1)S(1)}, s16[400,256]{1,0:T(8,128)(2,1)S(1)}, u32[]{:S(2)}, u32[]{:S(2)}) collective-permute-start(s16[400,256]{1,0:T(8,128)(2,1)S(1)} %get-tuple-element.36), channel_id=1, source_target_pairs={{0,64},{64,128},{128,192},{192,0},{1,65},{65,129},{129,193},{193,1... | collective-permute-start | bytes 614408 | tf_op jit(solution)/shard_map/ppermute | solution.py:246
  97.9 8.6 %collective-permute-start.14 = (s16[400,256]{1,0:T(8,128)(2,1)S(1)}, s16[400,256]{1,0:T(8,128)(2,1)S(1)}, u32[]{:S(2)}, u32[]{:S(2)}) collective-permute-start(s16[400,256]{1,0:T(8,128)(2,1)S(1)} %get-tuple-element.37), channel_id=1, source_target_pairs={{0,192},{64,0},{128,64},{192,128},{1,193},{65,1},{129,65},{193,129... | collective-permute-start | bytes 614408 | tf_op jit(solution)/shard_map/ppermute | solution.py:246
  107.6 18.9 %copy-start.1 = (f32[768,256]{1,0:T(8,128)S(1)}, f32[768,256]{1,0:T(8,128)}, u32[]{:S(2)}) copy-start(f32[768,256]{1,0:T(8,128)} %copy-done) | copy-start | bytes 2359300
  109.6 0.8 copy-start.3
  110.4 0.8 copy-start.5
  111.2 27.3 %collective-permute-start.18 = (s16[208,1024]{1,0:T(8,128)(2,1)}, s16[208,1024]{1,0:T(8,128)(2,1)}, u32[]{:S(2)}, u32[]{:S(2)}) collective-permute-start(s16[208,1024]{1,0:T(8,128)(2,1)} %get-tuple-element.43), channel_id=1, source_target_pairs={{0,2},{2,0},{4,6},{6,4},{1,3},{3,1},{5,7},{7,5},{8,10},{10,8},{12,... | collective-permute-start | bytes 1277960 | tf_op jit(solution)/shard_map/ppermute | solution.py:250
  112.4 11.0 %collective-permute-start.17 = (s16[784,256]{1,0:T(8,128)(2,1)}, s16[784,256]{1,0:T(8,128)(2,1)S(1)}, u32[]{:S(2)}, u32[]{:S(2)}) collective-permute-start(s16[784,256]{1,0:T(8,128)(2,1)} %get-tuple-element.42), channel_id=1, source_target_pairs={{0,192},{64,0},{128,64},{192,128},{1,193},{65,1},{129,65},{193,129... | collective-permute-start | bytes 1204232 | tf_op jit(solution)/shard_map/ppermute | solution.py:246
  115.3 11.2 %collective-permute-start.16 = (s16[784,256]{1,0:T(8,128)(2,1)S(1)}, s16[784,256]{1,0:T(8,128)(2,1)S(1)}, u32[]{:S(2)}, u32[]{:S(2)}) collective-permute-start(s16[784,256]{1,0:T(8,128)(2,1)S(1)} %get-tuple-element.38.after), channel_id=1, source_target_pairs={{0,64},{64,128},{128,192},{192,0},{1,65},{65,129},{129,193},{193,1... | collective-permute-start | bytes 1204232 | tf_op jit(solution)/shard_map/ppermute | solution.py:246
  126.5 9.7 %copy-start.6 = (s16[208,1024]{1,0:T(8,128)(2,1)S(1)}, s16[208,1024]{1,0:T(8,128)(2,1)}, u32[]{:S(2)}) copy-start(s16[208,1024]{1,0:T(8,128)(2,1)} %copy-done.5) | copy-start | bytes 1277956
  126.5 10.7 %copy-start.4 = (s16[208,1024]{1,0:T(8,128)(2,1)S(1)}, s16[208,1024]{1,0:T(8,128)(2,1)}, u32[]{:S(2)}) copy-start(s16[208,1024]{1,0:T(8,128)(2,1)} %copy-done.3) | copy-start | bytes 1277956
  127.6 37.0 %all-to-all-start.1 = ((s16[8,208,128]{2,1,0:T(8,128)(2,1)}), s16[8,208,128]{2,1,0:T(8,128)(2,1)S(1)}, u32[]{:S(2)}, u32[]{:S(2)}) async-start(s16[8,208,128]{2,1,0:T(8,128)(2,1)} %image_sum.1), calls=%async_computation.1 | async-start | bytes 851968 | tf_op jit(solution)/shard_map/all_to_all | solution.py:341
  136.2 20.3 %collective-permute-start.19 = (s16[208,1024]{1,0:T(8,128)(2,1)S(1)}, s16[208,1024]{1,0:T(8,128)(2,1)S(1)}, u32[]{:S(2)}, u32[]{:S(2)}) collective-permute-start(s16[208,1024]{1,0:T(8,128)(2,1)S(1)} %copy-done.6), channel_id=1, source_target_pairs={{0,4},{2,6},{4,0},{6,2},{1,5},{3,7},{5,1},{7,3},{8,12},{10,14},{12... | collective-permute-start | bytes 1277960 | tf_op jit(solution)/shard_map/ppermute | solution.py:250
  137.2 26.0 %collective-permute-start.20 = (s16[208,1024]{1,0:T(8,128)(2,1)S(1)}, s16[208,1024]{1,0:T(8,128)(2,1)S(1)}, u32[]{:S(2)}, u32[]{:S(2)}) collective-permute-start(s16[208,1024]{1,0:T(8,128)(2,1)S(1)} %copy-done.4), channel_id=1, source_target_pairs={{0,6},{2,4},{4,2},{6,0},{1,7},{3,5},{5,3},{7,1},{8,14},{10,12},{12... | collective-permute-start | bytes 1277960 | tf_op jit(solution)/shard_map/ppermute | solution.py:250
